TPU v7x, 32 devices: a whole 2x2x4 slice. The times are simulated.
32 devices in a mesh: grp: 4 (over y, x), col: 8 (over z, core).
Axes of the slice: x: 2, y: 2, z: 4, core: 2. Of those that a mesh axis runs over, the one named last changes fastest.
Arguments:
- inputs: bfloat16 [24, 256, 8192], P('grp', 'col'), may hold values from -6 to 6
- out_grads: bfloat16 [24, 256, 8192], P('grp', None, 'col'), may hold values from -0.5 to 0.5
- first_moment: float32 [8192, 8192], P(None, 'col'), may hold values from -2 to 2
- second_moment: float32 [8192, 8192], P(None, 'col'), may hold values from 0.01 to 1
- signs_in: int32 [8192], replicated, may hold values from 0 to 1
- signs_out: int32 [8192], replicated, may hold values from 0 to 1
- rows_in: int32 [64], replicated, may hold values from 0 to 8191, as said below
- rows_out: int32 [128], replicated, may hold values from 0 to 8191, as said below
- task_ids: int32 [24], P('grp'), may hold values from 0 to 7
- weights: int32 [24], P('grp'), may hold values from 1 to 4
Outputs:
- prototypes: float32 [8, 64, 128], P('grp', 'col')
Inputs may be any that keep to these rules, and one draw needn't show every extreme that they name: `rows_in`: distinct row numbers. `rows_out`: distinct row numbers.
All inputs are finite; a program needn't handle non-finite values.
Results may differ from a plain program's by a relative error of at most 0.0019.
Values may be sent and summed in bfloat16 or wider, within the bound.
No kernel may reach another device: no remote copies, remote signals or barrier semaphores. Data moves between devices by JAX's collectives and lax.ppermute only.
A program may use at most 256 MiB of HBM per device.

v0:
```python
import jax
import jax.numpy as jnp
from jax import lax
from jax.experimental import pallas as pl
from jax.experimental.pallas import tpu as pltpu
from jax.sharding import PartitionSpec as P

PRO_GRP = 2
BLOCK = 512
TILE = 256


def signed_hadamard(rows, cols, sign_bits):
    parity = lax.population_count(jnp.bitwise_and(rows, cols)) + sign_bits
    return (1 - 2 * jnp.bitwise_and(parity, 1)).astype(jnp.bfloat16)


def sketch_kernel(
    x_ref, og_ref, first_ref, second_ref, left_ref, right_ref, out_ref,
    first_s, second_s, xt_0, xt_1, g_0, g_1, u_0, u_1, t_0, t_1,
):
    xt_s, g_s, u_s, t_s = (xt_0, xt_1), (g_0, g_1), (u_0, u_1), (t_0, t_1)
    examples, _, cols = og_ref.shape
    n_right = right_ref.shape[1]
    tile = g_0.shape[1]

    @pl.when(pl.program_id(0) == 0)
    def _():
        out_ref[...] = jnp.zeros_like(out_ref)

    first_s[...] = 9.0 * first_ref[...]
    second_s[...] = 99.9 * second_ref[...]
    items = [(e, c) for e in range(examples) for c in range(0, cols, tile)]

    def make_grad(i):
        e, c = items[i]
        if c == 0:
            xt_s[e % 2][...] = x_ref[e].T
        g_s[i % 2][...] = jnp.dot(
            xt_s[e % 2][...], og_ref[e, :, c : c + tile], preferred_element_type=jnp.float32
        )

    def make_update(i):
        e, c = items[i]
        g = g_s[i % 2][...]
        first = first_s[:, c : c + tile] + g
        second = second_s[:, c : c + tile] + (0.1 * g) * g
        bottom = second * lax.rsqrt(second) + 1e-07
        u_s[e % 2][:, c : c + tile] = (first * pl.reciprocal(bottom, approx=True)).astype(
            jnp.bfloat16
        )

    def times_right(i):
        e, c = items[i]
        t = jnp.dot(
            u_s[e % 2][:, c : c + tile],
            right_ref[c : c + tile, :],
            preferred_element_type=jnp.float32,
        )
        if c == 0:
            t_s[e % 2][...] = t
        else:
            t_s[e % 2][...] += t

    def times_left(i):
        e, c = items[i]
        if c + tile != cols:
            return
        t = t_s[e % 2][...]
        high = t.astype(jnp.bfloat16)
        low = (t - high.astype(jnp.float32)).astype(jnp.bfloat16)
        both = jnp.dot(
            left_ref[...],
            jnp.concatenate([high, low], axis=1),
            preferred_element_type=jnp.float32,
        )
        out_ref[e] += both[:, :n_right] + both[:, n_right:]

    stages = (make_grad, make_update, times_right, times_left)
    for step in range(len(items) + len(stages) - 1):
        for lag, stage in enumerate(stages):
            if 0 <= step - lag < len(items):
                stage(step - lag)


def piece_sketch(gathered, out_grads, first, second, left, right, first_example, start):
    examples, tokens, rows = gathered.shape
    cols = out_grads.shape[2]
    n_left, n_right = left.shape[0], right.shape[1]
    block = min(BLOCK, rows)
    tile = min(TILE, cols)
    at = start // block
    group = first_example // examples
    elements = examples * rows * cols
    return pl.pallas_call(
        sketch_kernel,
        grid=(rows // block,),
        in_specs=[
            pl.BlockSpec((examples, tokens, block), lambda i: (0, 0, i)),
            pl.BlockSpec((examples, tokens, cols), lambda i: (group, 0, 0)),
            pl.BlockSpec((block, cols), lambda i: (i + at, 0)),
            pl.BlockSpec((block, cols), lambda i: (i + at, 0)),
            pl.BlockSpec((n_left, block), lambda i: (0, i + at)),
            pl.BlockSpec((cols, n_right), lambda i: (0, 0)),
        ],
        out_specs=pl.BlockSpec((examples, n_left, n_right), lambda i: (0, 0, 0)),
        out_shape=jax.ShapeDtypeStruct((examples, n_left, n_right), jnp.float32),
        scratch_shapes=[pltpu.VMEM((block, cols), jnp.float32)] * 2
        + [pltpu.VMEM((block, tokens), jnp.bfloat16)] * 2
        + [pltpu.VMEM((block, tile), jnp.float32)] * 2
        + [pltpu.VMEM((block, cols), jnp.bfloat16)] * 2
        + [pltpu.VMEM((block, n_right), jnp.float32)] * 2,
        compiler_params=pltpu.CompilerParams(
            vmem_limit_bytes=48 * 1024 * 1024, dimension_semantics=("arbitrary",)
        ),
        cost_estimate=pl.CostEstimate(
            flops=2 * elements * (tokens + n_right),
            bytes_accessed=2 * rows * cols * 4,
            transcendentals=2 * elements,
        ),
        name="piece_sketch",
    )(gathered, out_grads, first, second, left, right)


def pair_sum(value, axis, size):
    bit = 1
    while bit < size:
        value = value + lax.ppermute(value, axis, [(i, i ^ bit) for i in range(size)])
        bit *= 2
    return value


def body(
    inputs,
    out_grads,
    first_moment,
    second_moment,
    signs_in,
    signs_out,
    rows_in,
    rows_out,
    task_ids,
    weights,
):
    width, local_cols = first_moment.shape
    n_col = lax.axis_size("col")
    n_grp = lax.axis_size("grp")
    me_col = lax.axis_index("col")
    left = signed_hadamard(
        rows_in[:, None], jnp.arange(width, dtype=jnp.int32)[None, :], signs_in[None, :]
    )
    offset = me_col * local_cols
    mine = offset + jnp.arange(local_cols, dtype=jnp.int32)
    signs_mine = lax.dynamic_slice_in_dim(signs_out, offset, local_cols, 0)
    right = signed_hadamard(rows_out[None, :], mine[:, None], signs_mine[:, None])
    examples = inputs.shape[0]
    early = examples * 2 // 3
    most = width * 3 // 4
    pieces = [
        (0, early, 0, width),
        (early, examples - early, 0, most),
        (early, examples - early, most, width - most),
    ]
    sources = [inputs[e : e + n, :, r : r + rows] for e, n, r, rows in pieces]
    left, sources[1] = lax.optimization_barrier((left, sources[1]))
    gathered, parts = [], []
    for i, (e, n, r, rows) in enumerate(pieces):
        if i >= 2:
            gathered[i - 2], sources[i] = lax.optimization_barrier((gathered[i - 2], sources[i]))
        gathered.append(lax.all_gather(sources[i], "col", axis=1, tiled=True))
    for i, (e, n, r, rows) in enumerate(pieces):
        if i >= 1:
            parts[i - 1], gathered[i] = lax.optimization_barrier((parts[i - 1], gathered[i]))
        if i == 2:
            sketch, gathered[i] = lax.optimization_barrier((sketch, gathered[i]))
        parts.append(
            piece_sketch(gathered[i], out_grads, first_moment, second_moment, left, right, e, r)
        )
        if i == 1:
            sketch = pair_sum(parts[0], "col", n_col)
    sketch = jnp.concatenate([sketch, pair_sum(parts[1] + parts[2], "col", n_col)])
    squares = jnp.sum(sketch * sketch, axis=(1, 2))
    entries = sketch.shape[1] * sketch.shape[2]
    owned = sketch.shape[1] // n_col
    unit = lax.dynamic_slice_in_dim(sketch, me_col * owned, owned, 1)
    unit = unit * lax.rsqrt(squares / entries + 1e-06)[:, None, None]
    protos = jnp.arange(PRO_GRP * n_grp, dtype=jnp.int32)
    coef = jnp.where(
        task_ids[:, None] == protos[None, :], weights[:, None].astype(jnp.float32), 0.0
    )
    term = jnp.sum(coef[:, :, None, None] * unit[:, None], axis=0)
    term = pair_sum(term, "grp", n_grp)
    return lax.dynamic_slice_in_dim(term, lax.axis_index("grp") * PRO_GRP, PRO_GRP, 0)


def solution(mesh):
    placed = (
        P("grp", "col", None),
        P("grp", None, "col"),
        P(None, "col"),
        P(None, "col"),
        P(),
        P(),
        P(),
        P(),
        P("grp"),
        P("grp"),
    )
    return jax.shard_map(
        body, mesh=mesh, in_specs=placed, out_specs=P("grp", "col", None), check_vma=False
    )
```

profile of v0, /device:TPU:0, one launch (start us, length us, event | category | flops | bytes accessed | tf_op | source)
XLA Modules:
  0.0 324.7 jit_solution(9225859131067881362)
XLA Ops:
  6.5 3.1 slice.9
  9.8 2.2 slice.11
  12.0 1.6 subtract_convert_fusion.left_ref
  13.7 1.7 slice.10
  15.4 0.7 dynamic_slice.9
  16.1 147.6 %all-gather.4.cloned.1.call-done.x_ref = bf16[4,256,8192]{2,1,0:T(8,128)(2,1)} async-done(((bf16[4,32,8192]{2,1,0:T(8,128)(2,1)}), bf16[4,256,8192]{2,1,0:T(8,128)(2,1)}) %all-gather.4.cloned.1.call-update) | async-done | bytes 16777232 | tf_op jit(solution)/shard_map/all_gather | solution.py:170
  164.1 1.2 copy-done.1
  165.3 69.7 %piece_sketch.3 = f32[4,64,128]{2,1,0:T(8,128)S(1)} custom-call(bf16[4,256,8192]{2,1,0:T(8,128)(2,1)} %all-gather.4.cloned.1.call-done.x_ref, bf16[6,256,1024]{2,1,0:T(8,128)(2,1)S(1)} %copy-done, f32[8192,1024]{1,0:T(8,128)} %first_ref.5, f32[8192,1024]{1,0:T(8,128)} %second_ref.5, bf16[64,8192]{1,0:T(8,128)(2,1)S(1)} %copy-done.1, ...), custom_call_target="tpu_custom_call" | custom-call | flops 25769803776 | bytes 67108864 | tf_op jit(solution)/shard_map/piece_sketch/pallas_call | solution.py:95
  235.4 1.1 collective-permute-done
  236.5 13.4 %collective-permute-done.1 = f32[4,64,128]{2,1,0:T(8,128)S(1)} collective-permute-done((f32[4,64,128]{2,1,0:T(8,128)S(1)}, f32[4,64,128]{2,1,0:T(8,128)S(1)}, u32[]{:S(2)}, u32[]{:S(2)}) %collective-permute-start.1) | collective-permute-done | bytes 131104 | tf_op jit(solution)/shard_map/ppermute | solution.py:128
  250.0 1.2 copy-done.2
  251.2 31.6 %piece_sketch.4 = f32[2,64,128]{2,1,0:T(8,128)S(1)} custom-call(bf16[2,256,6144]{2,1,0:T(8,128)(2,1)} %all-gather.6.cloned.1.call-done.x_ref, bf16[6,256,1024]{2,1,0:T(8,128)(2,1)S(1)} %copy-done, f32[8192,1024]{1,0:T(8,128)} %first_ref.5, f32[8192,1024]{1,0:T(8,128)} %second_ref.5, bf16[64,8192]{1,0:T(8,128)(2,1)S(1)} %copy-done.2, ...), custom_call_target="tpu_custom_call" | custom-call | flops 9663676416 | bytes 50331648 | tf_op jit(solution)/shard_map/piece_sketch/pallas_call | solution.py:95
  282.9 1.2 copy-done.3
  284.1 1.6 copy-done.4
  285.7 12.3 %piece_sketch.5 = f32[2,64,128]{2,1,0:T(8,128)S(1)} custom-call(bf16[2,256,2048]{2,1,0:T(8,128)(2,1)S(1)} %copy-done.4, bf16[6,256,1024]{2,1,0:T(8,128)(2,1)} %og_ref.5, f32[8192,1024]{1,0:T(8,128)} %first_ref.5, f32[8192,1024]{1,0:T(8,128)} %second_ref.5, bf16[64,8192]{1,0:T(8,128)(2,1)S(1)} %copy-done.3, bf16[1024,128]{1,0:T(8,128)(2,1)S(1)} %subtract_convert_fusion.1.right_ref), custom_call_target="tpu_custom_call" | custom-call | flops 3221225472 | bytes 16777216 | tf_op jit(solution)/shard_map/piece_sketch/pallas_call | solution.py:95
  298.1 1.2 collective-permute-done.3
  299.5 4.2 %collective-permute-done.4 = f32[2,64,128]{2,1,0:T(8,128)S(1)} collective-permute-done((f32[2,64,128]{2,1,0:T(8,128)S(1)}, f32[2,64,128]{2,1,0:T(8,128)S(1)}, u32[]{:S(2)}, u32[]{:S(2)}) %collective-permute-start.4) | collective-permute-done | bytes 65568 | tf_op jit(solution)/shard_map/ppermute | solution.py:128
  303.7 3.0 collective-permute-start.5
  306.8 2.6 collective-permute-done.5
  309.7 1.5 collective-permute-start.6
  311.2 2.5 collective-permute-done.6
  313.7 1.5 collective-permute-start.7
  315.2 2.5 collective-permute-done.7
  317.6 0.6 dynamic-slice_add_fusion
  (46 shorter events, 1.7 us)
Async XLA Ops:
  6.5 157.1 %all-gather.4.cloned.1.call-start = ((), (), s32[]{:S(2)}) async-start(), calls=%async_computation | async-start | bytes 18874368 | tf_op jit(solution)/shard_map/all_gather | solution.py:170
  9.7 2.3 copy-start.5
  9.7 2.3 copy-start.6
  9.7 154.0 %copy-start.7 = (s32[128]{0:T(128)S(1)}, s32[128]{0:T(128)}, u32[]{:S(2)}) copy-start(s32[128]{0:T(128)} %param.17) | copy-start | bytes 1540
  9.7 154.3 %copy-start = (bf16[6,256,1024]{2,1,0:T(8,128)(2,1)S(1)}, bf16[6,256,1024]{2,1,0:T(8,128)(2,1)}, u32[]{:S(2)}) copy-start(bf16[6,256,1024]{2,1,0:T(8,128)(2,1)} %og_ref.5) | copy-start | bytes 9437188
  9.7 225.3 %all-gather.6.cloned.1.call-start = ((), (), s32[]{:S(2)}) async-start(), calls=%async_computation.1 | async-start | bytes 7077888 | tf_op jit(solution)/shard_map/all_gather | solution.py:170
  13.7 269.2 %all-gather.8.cloned.1.call-start = ((), (), s32[]{:S(2)}) async-start(), calls=%async_computation.2 | async-start | bytes 2359296 | tf_op jit(solution)/shard_map/all_gather | solution.py:170
  164.1 1.2 copy-start.1
  235.0 1.4 collective-permute-start
  236.5 13.5 %collective-permute-start.1 = (f32[4,64,128]{2,1,0:T(8,128)S(1)}, f32[4,64,128]{2,1,0:T(8,128)S(1)}, u32[]{:S(2)}, u32[]{:S(2)}) collective-permute-start(f32[4,64,128]{2,1,0:T(8,128)S(1)} %add.76), channel_id=1, source_target_pairs={{0,2},{1,3},{2,0},{3,1},{4,6},{5,7},{6,4},{7,5},{8,10},{9,11},{10,... | collective-permute-start | bytes 393224 | tf_op jit(solution)/shard_map/ppermute | solution.py:128
  249.9 32.9 %collective-permute-start.2 = (f32[4,64,128]{2,1,0:T(8,128)S(1)}, f32[4,64,128]{2,1,0:T(8,128)S(1)}, u32[]{:S(2)}, u32[]{:S(2)}) collective-permute-start(f32[4,64,128]{2,1,0:T(8,128)S(1)} %add.77), channel_id=1, source_target_pairs={{0,4},{1,5},{2,6},{3,7},{4,0},{5,1},{6,2},{7,3},{8,12},{9,13},{10,... | collective-permute-start | bytes 393224 | tf_op jit(solution)/shard_map/ppermute | solution.py:128
  250.0 1.2 copy-start.2
  282.9 1.2 copy-start.3
  284.1 1.6 copy-start.4
  285.7 13.8 %copy-start.9 = (s32[6]{0:T(128)S(1)}, s32[6]{0:T(128)}, u32[]{:S(2)}) copy-start(s32[6]{0:T(128)} %param.19) | copy-start | bytes 76
  285.7 21.0 %copy-start.8 = (s32[6]{0:T(128)S(1)}, s32[6]{0:T(128)}, u32[]{:S(2)}) copy-start(s32[6]{0:T(128)} %param.18) | copy-start | bytes 76
  298.0 1.3 collective-permute-start.3
  299.4 4.3 %collective-permute-start.4 = (f32[2,64,128]{2,1,0:T(8,128)S(1)}, f32[2,64,128]{2,1,0:T(8,128)S(1)}, u32[]{:S(2)}, u32[]{:S(2)}) collective-permute-start(f32[2,64,128]{2,1,0:T(8,128)S(1)} %add.80), channel_id=1, source_target_pairs={{0,2},{1,3},{2,0},{3,1},{4,6},{5,7},{6,4},{7,5},{8,10},{9,11},{10,... | collective-permute-start | bytes 196616 | tf_op jit(solution)/shard_map/ppermute | solution.py:128
  303.7 5.6 %collective-permute-start.5 = (f32[2,64,128]{2,1,0:T(8,128)S(1)}, f32[2,64,128]{2,1,0:T(8,128)S(1)}, u32[]{:S(2)}, u32[]{:S(2)}) collective-permute-start(f32[2,64,128]{2,1,0:T(8,128)S(1)} %add.81), channel_id=1, source_target_pairs={{0,4},{1,5},{2,6},{3,7},{4,0},{5,1},{6,2},{7,3},{8,12},{9,13},{10,... | collective-permute-start | bytes 196616 | tf_op jit(solution)/shard_map/ppermute | solution.py:128
  309.7 4.0 %collective-permute-start.6 = (f32[8,8,128]{2,1,0:T(8,128)S(1)}, f32[8,8,128]{2,1,0:T(8,128)S(1)}, u32[]{:S(2)}, u32[]{:S(2)}) collective-permute-start(f32[8,8,128]{2,1,0:T(8,128)S(1)} %multiply_reduce_fusion), channel_id=1, source_target_pairs={{0,8},{8,0},{16,24},{24,16},{1,9},{9,1},{17,25},{25,17},{2,10},{10... | collective-permute-start | bytes 98312 | tf_op jit(solution)/shard_map/ppermute | solution.py:128
  313.7 3.9 %collective-permute-start.7 = (f32[8,8,128]{2,1,0:T(8,128)S(1)}, f32[8,8,128]{2,1,0:T(8,128)S(1)}, u32[]{:S(2)}, u32[]{:S(2)}) collective-permute-start(f32[8,8,128]{2,1,0:T(8,128)S(1)} %add.85), channel_id=1, source_target_pairs={{0,16},{8,24},{16,0},{24,8},{1,17},{9,25},{17,1},{25,9},{2,18},{10... | collective-permute-start | bytes 98312 | tf_op jit(solution)/shard_map/ppermute | solution.py:128
Sparse Core Ops, SparseCore 0:
  9.8 153.7 all-gather.3
  165.3 62.8 all-gather.5
  229.8 34.8 all-gather.7
where the time goes:
time: 325 us
  waiting for transfers between devices  175 us (54%)
  Pallas kernels  114 us (35%)
  between operations  13.3 us (4%)
  local copies, waits for them, and re-layouts  13 us (4%)
  starting transfers between devices  6.63 us (2%)
    all_gather x3, waiting for transfers between devices, body(): gathered.append(lax.all_gather(sources[i], 'col', axis=1, tiled=True))  148 us
    pallas_call x3, Pallas kernels, piece_sketch(): pl.pallas_call(sketch_kernel, grid=(rows // block,), in_specs=[pl.BlockSp...  114 us
    ppermute x8, waiting for transfers between devices, pair_sum(): lax.ppermute(value, axis, [(i, i ^ bit) for i in range(size)])  27.5 us
    slice x3, local copies, waits for them, and re-layouts, body(): sources = [inputs[e:e + n, :, r:r + rows] for e, n, r, rows in pieces]  7.02 us
    ppermute x8, starting transfers between devices, pair_sum(): lax.ppermute(value, axis, [(i, i ^ bit) for i in range(size)])  6.55 us
  transfers between devices with their start and end apart: 11, of which 8 were waited for; matrix products, arithmetic and copies ran while one was open for 2% of the time, Pallas kernels for 31%

commit v1 on v0

--- a/solution.py
+++ b/solution.py
@@ -122,8 +122,7 @@
     )(gathered, out_grads, first, second, left, right)
 
 
-def pair_sum(value, axis, size):
-    bit = 1
+def pair_sum(value, axis, size, bit=1):
     while bit < size:
         value = value + lax.ppermute(value, axis, [(i, i ^ bit) for i in range(size)])
         bit *= 2
@@ -153,37 +152,31 @@
     mine = offset + jnp.arange(local_cols, dtype=jnp.int32)
     signs_mine = lax.dynamic_slice_in_dim(signs_out, offset, local_cols, 0)
     right = signed_hadamard(rows_out[None, :], mine[:, None], signs_mine[:, None])
-    examples = inputs.shape[0]
-    early = examples * 2 // 3
-    most = width * 3 // 4
-    pieces = [
-        (0, early, 0, width),
-        (early, examples - early, 0, most),
-        (early, examples - early, most, width - most),
-    ]
-    sources = [inputs[e : e + n, :, r : r + rows] for e, n, r, rows in pieces]
+    pieces = [(0, width // 2), (width // 2, 3 * width // 8), (7 * width // 8, width // 8)]
+    sources = [inputs[:, :, r : r + rows] for r, rows in pieces]
     left, sources[1] = lax.optimization_barrier((left, sources[1]))
     gathered, parts = [], []
-    for i, (e, n, r, rows) in enumerate(pieces):
+    for i in range(len(pieces)):
         if i >= 2:
             gathered[i - 2], sources[i] = lax.optimization_barrier((gathered[i - 2], sources[i]))
         gathered.append(lax.all_gather(sources[i], "col", axis=1, tiled=True))
-    for i, (e, n, r, rows) in enumerate(pieces):
+    for i, (r, rows) in enumerate(pieces):
         if i >= 1:
             parts[i - 1], gathered[i] = lax.optimization_barrier((parts[i - 1], gathered[i]))
-        if i == 2:
-            sketch, gathered[i] = lax.optimization_barrier((sketch, gathered[i]))
         parts.append(
-            piece_sketch(gathered[i], out_grads, first_moment, second_moment, left, right, e, r)
-        )
-        if i == 1:
-            sketch = pair_sum(parts[0], "col", n_col)
-    sketch = jnp.concatenate([sketch, pair_sum(parts[1] + parts[2], "col", n_col)])
-    squares = jnp.sum(sketch * sketch, axis=(1, 2))
-    entries = sketch.shape[1] * sketch.shape[2]
-    owned = sketch.shape[1] // n_col
-    unit = lax.dynamic_slice_in_dim(sketch, me_col * owned, owned, 1)
-    unit = unit * lax.rsqrt(squares / entries + 1e-06)[:, None, None]
+            piece_sketch(gathered[i], out_grads, first_moment, second_moment, left, right, 0, r)
+        )
+    sketch = sum(parts)
+    examples, n_left, n_right = sketch.shape
+    owned = n_left // n_col
+    sketch = sketch + lax.ppermute(sketch, "col", [(i, i ^ 1) for i in range(n_col)])
+    sketch = sketch.reshape(examples, n_col // 2, 2, owned, n_right)
+    sketch = lax.dynamic_index_in_dim(sketch, me_col % 2, 2, keepdims=False)
+    sketch = pair_sum(sketch, "col", n_col, 2)
+    squares = jnp.sum(sketch * sketch, axis=(1, 2, 3))
+    squares = squares + lax.ppermute(squares, "col", [(i, i ^ 1) for i in range(n_col)])
+    unit = lax.dynamic_index_in_dim(sketch, me_col // 2, 1, keepdims=False)
+    unit = unit * lax.rsqrt(squares / (n_left * n_right) + 1e-06)[:, None, None]
     protos = jnp.arange(PRO_GRP * n_grp, dtype=jnp.int32)
     coef = jnp.where(
         task_ids[:, None] == protos[None, :], weights[:, None].astype(jnp.float32), 0.0

time: 325 us -> 310 us (0.954)
  Pallas kernels: 114 us -> 105 us
  waiting for transfers between devices: 175 us -> 169 us
    ppermute x8 -> x4, waiting for transfers between devices: 27.5 us -> 16 us  [pair_sum(): lax.ppermute(value, axis, [(i, i ^ bit) for i in range(size)])]
    pallas_call x3, Pallas kernels: 114 us -> 105 us  [piece_sketch(): pl.pallas_call(sketch_kernel, grid=(rows // block,), in_specs=[pl.BlockSp...]
    ppermute x8 -> x4, starting transfers between devices: 6.55 us -> 4.02 us  [pair_sum(): lax.ppermute(value, axis, [(i, i ^ bit) for i in range(size)])]
    unnamed x20 -> x28, local copies, waits for them, and re-layouts: 5.27 us -> 6.94 us
  transfers between devices with their start and end apart: 11 -> 9, of which waited for: 8 -> 8; matrix products, arithmetic and copies ran while one was open for 2% -> 2% of each run, Pallas kernels for 31% -> 29%
where the time goes in v1:
time: 310 us; the launch traced here: 309 us
  waiting for transfers between devices  169 us (55%)
  Pallas kernels  105 us (34%)
  local copies, waits for them, and re-layouts  14.6 us (5%)
  between operations  13.3 us (4%)
  starting transfers between devices  4.47 us (1%)
    all_gather x3, waiting for transfers between devices, body(): gathered.append(lax.all_gather(sources[i], 'col', axis=1, tiled=True))  150 us
    pallas_call x3, Pallas kernels, piece_sketch(): pl.pallas_call(sketch_kernel, grid=(rows // block,), in_specs=[pl.BlockSp...  105 us
    ppermute x4, waiting for transfers between devices, pair_sum(): lax.ppermute(value, axis, [(i, i ^ bit) for i in range(size)])  16 us
    slice x3, local copies, waits for them, and re-layouts, body(): sources = [inputs[:, :, r:r + rows] for r, rows in pieces]  6.98 us
    unnamed x28, local copies, waits for them, and re-layouts  6.94 us
  transfers between devices with their start and end apart: 9, of which 8 were waited for; matrix products, arithmetic and copies ran while one was open for 2% of the time, Pallas kernels for 29%

profile of v1, /device:TPU:0, one launch (start us, length us, event | category | flops | bytes accessed | tf_op | source)
XLA Modules:
  0.0 309.4 jit_solution(2676291753840371006)
XLA Ops:
  6.5 2.7 slice.9
  9.3 2.5 slice.11
  11.8 1.6 subtract_convert_fusion.left_ref
  13.5 1.8 slice.10
  15.3 113.6 %all-gather.4.cloned.1.call-done.x_ref = bf16[6,256,4096]{2,1,0:T(8,128)(2,1)} async-done(((bf16[6,32,4096]{2,1,0:T(8,128)(2,1)}), bf16[6,256,4096]{2,1,0:T(8,128)(2,1)}) %all-gather.4.cloned.1.call-update) | async-done | bytes 12582928 | tf_op jit(solution)/shard_map/all_gather | solution.py:162
  128.9 0.7 dynamic_slice.14
  130.0 1.2 copy-done.1
  131.2 50.9 %piece_sketch.3 = f32[6,64,128]{2,1,0:T(8,128)S(1)} custom-call(bf16[6,256,4096]{2,1,0:T(8,128)(2,1)} %all-gather.4.cloned.1.call-done.x_ref, bf16[6,256,1024]{2,1,0:T(8,128)(2,1)S(1)} %copy-done, f32[8192,1024]{1,0:T(8,128)} %first_ref.5, f32[8192,1024]{1,0:T(8,128)} %second_ref.5, bf16[64,8192]{1,0:T(8,128)(2,1)S(1)} %copy-done.1, ...), custom_call_target="tpu_custom_call" | custom-call | flops 19327352832 | bytes 33554432 | tf_op jit(solution)/shard_map/piece_sketch/pallas_call | solution.py:95
  182.8 36.6 %all-gather.6.cloned.1.call-done.x_ref = bf16[6,256,3072]{2,1,0:T(8,128)(2,1)} async-done(((bf16[6,32,3072]{2,1,0:T(8,128)(2,1)}), bf16[6,256,3072]{2,1,0:T(8,128)(2,1)}) %all-gather.6.cloned.1.call-update) | async-done | bytes 9437200 | tf_op jit(solution)/shard_map/all_gather | solution.py:162
  219.4 1.2 copy-done.2
  220.6 38.9 %piece_sketch.4 = f32[6,64,128]{2,1,0:T(8,128)S(1)} custom-call(bf16[6,256,3072]{2,1,0:T(8,128)(2,1)} %all-gather.6.cloned.1.call-done.x_ref, bf16[6,256,1024]{2,1,0:T(8,128)(2,1)S(1)} %copy-done, f32[8192,1024]{1,0:T(8,128)} %first_ref.5, f32[8192,1024]{1,0:T(8,128)} %second_ref.5, bf16[64,8192]{1,0:T(8,128)(2,1)S(1)} %copy-done.2, ...), custom_call_target="tpu_custom_call" | custom-call | flops 14495514624 | bytes 25165824 | tf_op jit(solution)/shard_map/piece_sketch/pallas_call | solution.py:95
  259.6 0.7 copy-done.5
  260.3 1.2 copy-done.3
  261.5 1.9 copy-done.4
  263.4 15.6 %piece_sketch.5 = f32[6,64,128]{2,1,0:T(8,128)S(1)} custom-call(bf16[6,256,1024]{2,1,0:T(8,128)(2,1)S(1)} %copy-done.4, bf16[6,256,1024]{2,1,0:T(8,128)(2,1)} %og_ref.5, f32[8192,1024]{1,0:T(8,128)} %first_ref.5, f32[8192,1024]{1,0:T(8,128)} %second_ref.5, bf16[64,8192]{1,0:T(8,128)(2,1)S(1)} %copy-done.3, bf16[1024,128]{1,0:T(8,128)(2,1)S(1)} %subtract_convert_fusion.1.right_ref), custom_call_target="tpu_custom_call" | custom-call | flops 4831838208 | bytes 8388608 | tf_op jit(solution)/shard_map/piece_sketch/pallas_call | solution.py:95
  279.4 1.2 collective-permute-done
  280.7 4.9 %collective-permute-done.1 = f32[6,4,8,128]{3,2,1,0:T(8,128)S(1)} collective-permute-done((f32[6,4,8,128]{3,2,1,0:T(8,128)S(1)}, f32[6,4,8,128]{3,2,1,0:T(8,128)S(1)}, u32[]{:S(2)}, u32[]{:S(2)}) %collective-permute-start.1) | collective-permute-done | bytes 98336 | tf_op jit(solution)/shard_map/ppermute | solution.py:127
  285.6 0.9 collective-permute-start.2
  286.7 6.2 %collective-permute-done.2 = f32[6,4,8,128]{3,2,1,0:T(8,128)S(1)} collective-permute-done((f32[6,4,8,128]{3,2,1,0:T(8,128)S(1)}, f32[6,4,8,128]{3,2,1,0:T(8,128)S(1)}, u32[]{:S(2)}, u32[]{:S(2)}) %collective-permute-start.2) | collective-permute-done | bytes 98336 | tf_op jit(solution)/shard_map/ppermute | solution.py:127
  293.0 1.1 collective-permute-done.3
  294.4 1.5 collective-permute-start.4
  295.9 2.4 collective-permute-done.4
  298.3 1.5 collective-permute-start.5
  299.8 2.4 collective-permute-done.5
  (47 shorter events, 2.7 us)
Async XLA Ops:
  6.5 122.3 %all-gather.4.cloned.1.call-start = ((), (), s32[]{:S(2)}) async-start(), calls=%async_computation | async-start | bytes 14155776 | tf_op jit(solution)/shard_map/all_gather | solution.py:162
  9.2 2.6 copy-start.9
  9.3 2.6 copy-start.10
  9.3 210.1 %all-gather.6.cloned.1.call-start = ((), (), s32[]{:S(2)}) async-start(), calls=%async_computation.1 | async-start | bytes 10616832 | tf_op jit(solution)/shard_map/all_gather | solution.py:162
  11.8 117.8 %copy-start.11 = (s32[128]{0:T(128)S(1)}, s32[128]{0:T(128)}, u32[]{:S(2)}) copy-start(s32[128]{0:T(128)} %param.17) | copy-start | bytes 1540
  11.8 118.1 %copy-start = (bf16[6,256,1024]{2,1,0:T(8,128)(2,1)S(1)}, bf16[6,256,1024]{2,1,0:T(8,128)(2,1)}, u32[]{:S(2)}) copy-start(bf16[6,256,1024]{2,1,0:T(8,128)(2,1)} %og_ref.5) | copy-start | bytes 9437188
  13.4 246.9 %all-gather.8.cloned.1.call-start = ((), (), s32[]{:S(2)}) async-start(), calls=%async_computation.2 | async-start | bytes 3538944 | tf_op jit(solution)/shard_map/all_gather | solution.py:162
  129.9 1.2 copy-start.1
  182.1 0.7 copy-start.7
  219.4 1.2 copy-start.2
  259.6 0.7 copy-start.5
  260.3 1.2 copy-start.3
  261.5 1.9 copy-start.4
  263.4 15.6 %copy-start.6 = (f32[6,64,128]{2,1,0:T(8,128)S(1)}, f32[6,64,128]{2,1,0:T(8,128)}, u32[]{:S(2)}) copy-start(f32[6,64,128]{2,1,0:T(8,128)} %copy-done.5) | copy-start | bytes 589828
  263.4 15.6 %copy-start.8 = (f32[6,64,128]{2,1,0:T(8,128)S(1)}, f32[6,64,128]{2,1,0:T(8,128)}, u32[]{:S(2)}) copy-start(f32[6,64,128]{2,1,0:T(8,128)} %copy-done.7) | copy-start | bytes 589828
  263.4 17.3 %copy-start.13 = (s32[6]{0:T(128)S(1)}, s32[6]{0:T(128)}, u32[]{:S(2)}) copy-start(s32[6]{0:T(128)} %param.19) | copy-start | bytes 76
  263.4 23.2 %copy-start.12 = (s32[6]{0:T(128)S(1)}, s32[6]{0:T(128)}, u32[]{:S(2)}) copy-start(s32[6]{0:T(128)} %param.18) | copy-start | bytes 76
  279.1 1.5 collective-permute-start
  280.6 5.0 %collective-permute-start.1 = (f32[6,4,8,128]{3,2,1,0:T(8,128)S(1)}, f32[6,4,8,128]{3,2,1,0:T(8,128)S(1)}, u32[]{:S(2)}, u32[]{:S(2)}) collective-permute-start(f32[6,4,8,128]{3,2,1,0:T(8,128)S(1)} %dynamic-slice_bitcast_fusion), channel_id=1, source_target_pairs={{0,2},{1,3},{2,0},{3,1},{4,6},{5,7},{6,4},{7,5},{8,10},{9,11},{10,... | collective-permute-start | bytes 294920 | tf_op jit(solution)/shard_map/ppermute | solution.py:127
  285.6 7.2 %collective-permute-start.2 = (f32[6,4,8,128]{3,2,1,0:T(8,128)S(1)}, f32[6,4,8,128]{3,2,1,0:T(8,128)S(1)}, u32[]{:S(2)}, u32[]{:S(2)}) collective-permute-start(f32[6,4,8,128]{3,2,1,0:T(8,128)S(1)} %fusion.1), channel_id=1, source_target_pairs={{0,4},{1,5},{2,6},{3,7},{4,0},{5,1},{6,2},{7,3},{8,12},{9,13},{10,... | collective-permute-start | bytes 294920 | tf_op jit(solution)/shard_map/ppermute | solution.py:127
  293.0 1.2 collective-permute-start.3
  294.4 4.0 %collective-permute-start.4 = (f32[8,8,128]{2,1,0:T(8,128)S(1)}, f32[8,8,128]{2,1,0:T(8,128)S(1)}, u32[]{:S(2)}, u32[]{:S(2)}) collective-permute-start(f32[8,8,128]{2,1,0:T(8,128)S(1)} %multiply_reduce_fusion), channel_id=1, source_target_pairs={{0,8},{8,0},{16,24},{24,16},{1,9},{9,1},{17,25},{25,17},{2,10},{10... | collective-permute-start | bytes 98312 | tf_op jit(solution)/shard_map/ppermute | solution.py:127
  298.3 3.9 %collective-permute-start.5 = (f32[8,8,128]{2,1,0:T(8,128)S(1)}, f32[8,8,128]{2,1,0:T(8,128)S(1)}, u32[]{:S(2)}, u32[]{:S(2)}) collective-permute-start(f32[8,8,128]{2,1,0:T(8,128)S(1)} %add.89), channel_id=1, source_target_pairs={{0,16},{8,24},{16,0},{24,8},{1,17},{9,25},{17,1},{25,9},{2,18},{10... | collective-permute-start | bytes 98312 | tf_op jit(solution)/shard_map/ppermute | solution.py:127
Sparse Core Ops, SparseCore 0:
  9.4 119.4 all-gather.3
  130.5 88.9 all-gather.5
  221.0 36.7 all-gather.7
